TPU v7x, 32 devices: a whole 2x2x4 slice. The times are simulated.
32 devices in a mesh: group: 2 (over y), dp: 4 (over z), tensor: 4 (over x, core).
Axes of the slice: x: 2, y: 2, z: 4, core: 2. Of those that a mesh axis runs over, the one named last changes fastest.
Arguments:
- tokens: bfloat16 [4096, 4096], P(('group', 'dp', 'tensor')), parts along dimension 0, may hold values from -6 to 6
- cotangent: bfloat16 [4096, 4096], P(('group', 'dp', 'tensor')), parts along dimension 0, may hold values from -0.13183594 to 0.13183594
- weights: bfloat16 [3, 4, 262144], P(None, None, ('dp', 'tensor')), may hold values from -0.125 to 0.125
- kept: int32 [2, 4, 16], replicated, may hold values from 0 to 31, as said below
Outputs:
- weight_grads: float32 [6, 4, 262144], P('group', None, ('dp', 'tensor')), parts along dimension 0
There are 2 independent parts, one for each index of `group`. A program takes and returns all parts, laid end to end along the dimension named above; an argument that names none is the same for every part. Nothing has to cross between parts.
Inputs may be any that keep to these rules, and one draw needn't show every extreme that they name: `kept`: each table row lists 16 distinct block indices.
All inputs are finite; a program needn't handle non-finite values.
Results may differ from a plain program's by a relative error of at most 0.0029.
Values may be sent and summed in bfloat16 or wider, within the bound.
A program may use at most 192 MiB of HBM per device.

v0:
```python
import jax
import jax.numpy as jnp
from jax import lax
from jax.sharding import PartitionSpec as P

BLK = 128


def per_device(tokens, cotangent, weights, kept):
    tok_rows, cot_rows = (
        lax.all_gather(tokens, "tensor", axis=0, tiled=True),
        lax.all_gather(cotangent, "tensor", axis=0, tiled=True),
    )
    tensor_size = lax.axis_size("tensor")
    dp_size = lax.axis_size("dp")
    tensor_rank = lax.axis_index("tensor")
    columns = weights.shape[1]
    cols_dev = columns // tensor_size
    slice_len = weights.shape[2]
    gathered = lax.all_gather(weights, "dp", axis=2, tiled=True)
    owned = lax.all_to_all(gathered, "tensor", split_axis=1, concat_axis=2, tiled=True)
    owned = owned.reshape(3, cols_dev, tensor_size, dp_size, slice_len)
    owned = jnp.transpose(owned, (0, 1, 3, 2, 4))
    blocks = owned.reshape(3, cols_dev, -1, BLK, BLK)
    tables = lax.dynamic_slice_in_dim(kept, tensor_rank * cols_dev, cols_dev, 1)
    row_count = tok_rows.shape[0]
    picked_x = jnp.take(tok_rows.reshape(row_count, -1, BLK), tables[0], axis=1)
    picked_y = jnp.take(cot_rows.reshape(row_count, -1, BLK), tables[1], axis=1)
    gate = jnp.einsum("rckb,ckbs->rcs", picked_x, blocks[0], preferred_element_type=jnp.float32)
    up_val = jnp.einsum("rckb,ckbs->rcs", picked_x, blocks[1], preferred_element_type=jnp.float32)
    sigmoid_gate = jax.nn.sigmoid(gate)
    silu_gate = gate * sigmoid_gate
    hidden = (silu_gate * up_val).astype(jnp.bfloat16)
    grad_hidden = jnp.einsum(
        "rcks,ckhs->rch", picked_y, blocks[2], preferred_element_type=jnp.float32
    )
    grad_gate = (grad_hidden * up_val * sigmoid_gate * (1.0 + gate * (1.0 - sigmoid_gate))).astype(
        jnp.bfloat16
    )
    grad_up = (grad_hidden * silu_gate).astype(jnp.bfloat16)
    gate_grad = jnp.einsum(
        "rckb,rcs->ckbs", picked_x, grad_gate, preferred_element_type=jnp.float32
    )
    up_grad = jnp.einsum("rckb,rcs->ckbs", picked_x, grad_up, preferred_element_type=jnp.float32)
    down_grad = jnp.einsum("rch,rcks->ckhs", hidden, picked_y, preferred_element_type=jnp.float32)
    partial_grads = jnp.stack([gate_grad, up_grad, down_grad]).reshape(3, cols_dev, -1)
    summed = lax.psum_scatter(partial_grads, "dp", scatter_dimension=2, tiled=True)
    home = lax.all_to_all(summed, "tensor", split_axis=2, concat_axis=1, tiled=True)
    return home


def solution(mesh):
    in_specs = (
        P(("group", "dp", "tensor"), None),
        P(("group", "dp", "tensor"), None),
        P(None, None, ("dp", "tensor")),
        P(),
    )
    out_specs = P("group", None, ("dp", "tensor"))
    return jax.shard_map(
        per_device, mesh=mesh, in_specs=in_specs, out_specs=out_specs, check_vma=False
    )
```

profile of v0, /device:TPU:0, one launch (start us, length us, event | category | flops | bytes accessed | tf_op | source)
XLA Modules:
  0.0 783.8 jit_solution(11926886368671847585)
XLA Ops:
  6.5 2.3 copy.54
  8.9 1.3 copy.50
  10.3 1.4 copy.52
  11.7 46.0 %all-gather.8.cloned.1.call-done = bf16[3,4,65536]{2,0,1:T(4,128)(2,1)} async-done(((bf16[3,4,16384]{2,0,1:T(4,128)(2,1)}), bf16[3,4,65536]{2,0,1:T(4,128)(2,1)}) %all-gather.8.cloned.1.call-update) | async-done | bytes 1572880 | tf_op jit(solution)/shard_map/all_gather | solution.py:20
  57.6 3.6 all-to-all-start
  61.3 0.7 and_bitcast_fusion.1
  62.0 43.8 %all-to-all-done = bf16[3,4,65536]{2,0,1:T(4,128)(2,1)S(1)} async-done(((bf16[3,4,65536]{2,0,1:T(4,128)(2,1)}), bf16[3,4,65536]{2,0,1:T(4,128)(2,1)S(1)}, u32[]{:S(2)}, u32[]{:S(2)}) %all-to-all-start) | async-done | bytes 1572896 | tf_op jit(solution)/shard_map/all_to_all | solution.py:21
  105.8 3.2 reshape.129
  109.0 2.1 copy.73
  114.0 1.3 reshape.92
  115.3 6.6 copy.51
  121.9 3.2 gather_fusion
  125.1 0.7 convolution_bitcast_fusion.1
  126.2 1.5 convolution_bitcast_fusion.2
  127.6 18.3 %all-gather.6.cloned.1.call-done = bf16[512,4096]{0,1:T(8,128)(2,1)} async-done(((bf16[128,4096]{0,1:T(8,128)(2,1)}), bf16[512,4096]{0,1:T(8,128)(2,1)}) %all-gather.6.cloned.1.call-update) | async-done | bytes 4194320 | tf_op jit(solution)/shard_map/all_gather | solution.py:12
  146.0 6.5 copy.53
  152.4 4.3 gather_fusion.1
  156.8 2.5 convolution_bitcast_fusion.3
  159.3 1.1 convolution_bitcast_fusion
  160.4 2.1 fusion.10
  162.5 2.1 fusion.6
  164.9 0.9 copy-done.3
  165.8 6.1 pad_maximum_fusion
  173.7 119.4 %all-reduce.3.cloned.1.call-done = f32[3,1,262144]{2,1,0:T(1,128)} async-done(((f32[3,1,262144]{2,1,0:T(1,128)}), f32[3,1,262144]{2,1,0:T(1,128)}) %all-reduce.3.cloned.1.call-update) | async-done | bytes 3145744
  293.1 1.2 constant_dynamic-slice_fusion
  294.3 47.6 %copy.63 = f32[3,1,65536]{0,1,2:T(1,128)} copy(f32[3,1,65536]{2,1,0:T(1,128)S(1)} %constant_dynamic-slice_fusion) | data formatting | bytes 1572864 | tf_op jit(solution)/shard_map/reduce_scatter | solution.py:47
  342.4 291.0 %reduce = f32[65536,3]{1,0:T(8,128)} reduce(f32[65536,1,3]{2,1,0:T(1,128)} %bitcast.103, f32[]{:T(128)} %broadcast.77), dimensions={1}, to_apply=%bitcast.95.reduce_sub_computation | reduce | bytes 1572868
  633.3 42.8 %reshape.133 = f32[4,1,49152]{2,1,0:T(1,128)S(1)} reshape(f32[65536,3]{1,0:T(8,128)} %reduce) | data formatting | bytes 1572864
  676.1 14.2 %all_to_all.21 = f32[4,1,49152]{2,1,0:T(1,128)S(1)} all-to-all(f32[4,1,49152]{2,1,0:T(1,128)S(1)} %reshape.133), channel_id=1, replica_groups=mesh['group'=2,'dp'=4,'tensor'=4] {'tensor'}, dimensions={0} | all-to-all | bytes 1572864 | tf_op jit(solution)/shard_map/all_to_all | solution.py:48
  690.3 2.9 reduce.1
  693.3 65.7 %reshape.134 = f32[65536,1,3]{2,1,0:T(1,128)} reshape(f32[4,49152]{1,0:T(4,128)S(1)} %reduce.1) | data formatting | bytes 1572864
  758.9 18.2 %copy.69 = f32[3,4,16384]{2,1,0:T(4,128)} copy(f32[3,4,16384]{0,2,1:T(8,128)} %bitcast.104) | data formatting | bytes 1572864 | tf_op jit(solution)/shard_map/all_to_all | solution.py:48
  (33 shorter events, 5.4 us)
Async XLA Ops:
  6.5 2.4 copy-start.1
  6.5 3.7 copy-start.2
  6.5 51.1 %all-gather.8.cloned.1.call-start = ((), (), s32[]{:S(2)}) async-start(), calls=%async_computation.4 | async-start | bytes 2621440 | tf_op jit(solution)/shard_map/all_gather | solution.py:20
  8.8 106.5 %all-gather.4.cloned.1.call-start = ((), (), s32[]{:S(2)}) async-start(), calls=%async_computation.2 | async-start | bytes 5242880 | tf_op jit(solution)/shard_map/all_gather | solution.py:11
  10.2 135.7 %all-gather.6.cloned.1.call-start = ((), (), s32[]{:S(2)}) async-start(), calls=%async_computation.3 | async-start | bytes 5242880 | tf_op jit(solution)/shard_map/all_gather | solution.py:12
  57.6 48.2 %all-to-all-start = ((bf16[3,4,65536]{2,0,1:T(4,128)(2,1)}), bf16[3,4,65536]{2,0,1:T(4,128)(2,1)S(1)}, u32[]{:S(2)}, u32[]{:S(2)}) async-start(bf16[3,4,65536]{2,0,1:T(4,128)(2,1)} %all-gather.8.cloned.1.call-done), calls=%async_computation | async-start | bytes 4194304 | tf_op jit(solution)/shard_map/all_to_all | solution.py:21
  61.2 231.9 %all-reduce.3.cloned.1.call-start = ((), (), s32[]{:S(2)}) async-start(), calls=%async_computation.5 | async-start | bytes 6291456
  125.1 1.0 copy-start.4
  156.8 2.5 copy-start
  156.8 2.5 copy-start.6
  164.6 1.2 copy-start.3
  171.8 0.7 copy-start.5
Sparse Core Ops, SparseCore 0:
  9.0 48.6 all-gather.7
  59.2 52.3 all-gather.3
  113.1 32.8 all-gather.5
  172.0 121.0 all-reduce.2
where the time goes:
time: 798 us; the launch traced here: 784 us
  other arithmetic  301 us (38%)
  waiting for transfers between devices  228 us (29%)
  local copies, waits for them, and re-layouts  214 us (27%)
  blocking collectives  14.2 us (2%)
  between operations  14.2 us (2%)
  matrix products  9.92 us (1%)
    unnamed x1, other arithmetic  291 us
    unnamed x5, waiting for transfers between devices  119 us
    unnamed x22, local copies, waits for them, and re-layouts  117 us
    reduce_scatter x1, local copies, waits for them, and re-layouts, per_device(): lax.psum_scatter(partial_grads, 'dp', scatter_dimension=2, tiled=True)  47.6 us
    all_gather x1, waiting for transfers between devices, per_device(): gathered = lax.all_gather(weights, 'dp', axis=2, tiled=True)  46 us
    all_to_all x1, waiting for transfers between devices, per_device(): lax.all_to_all(gathered, 'tensor', split_axis=1, concat_axis=2, tiled=True)  43.8 us
    all_gather x1, waiting for transfers between devices, per_device(): lax.all_gather(cotangent, 'tensor', axis=0, tiled=True)  18.3 us
    all_to_all x1, local copies, waits for them, and re-layouts, per_device(): lax.all_to_all(summed, 'tensor', split_axis=2, concat_axis=1, tiled=True)  18.2 us
  transfers between devices with their start and end apart: 5, of which 4 were waited for; matrix products, arithmetic and copies ran while one was open for 3% of the time, Pallas kernels for 0%

commit v1 on v0

v1 whole, which is shorter than its diff:
```python
import functools

import jax
import jax.numpy as jnp
from jax import lax
from jax.experimental import pallas as pl
from jax.experimental.pallas import tpu as pltpu
from jax.sharding import PartitionSpec as P

BLK = 128
MESH = pl.DeviceIdType.MESH
F32 = jnp.float32
BF16 = jnp.bfloat16


def activations(gate, up_val, grad_hidden):
    sigmoid_gate = jax.nn.sigmoid(gate)
    silu_gate = gate * sigmoid_gate
    hidden = (silu_gate * up_val).astype(BF16)
    grad_gate = (grad_hidden * up_val * sigmoid_gate * (1.0 + gate * (1.0 - sigmoid_gate))).astype(BF16)
    grad_up = (grad_hidden * silu_gate).astype(BF16)
    return hidden, grad_gate, grad_up


def fused_kernel(
    n_dp, n_tensor,
    kept_ref, tok_ref, cot_ref, w_ref, out_ref,
    tok_tiles, cot_tiles, pack, rows, owned, act, grads, parts,
    tok_send, tok_recv, hop_send, hop_recv, ring_send, ring_recv, grad_send, grad_recv,
):
    n_dev = n_dp * n_tensor
    keep = kept_ref.shape[2]
    tok_dev = tok_ref.shape[0]
    dp = lax.axis_index("dp")
    tensor = lax.axis_index("tensor")
    me = dp * n_tensor + tensor

    def device(index):
        return {"dp": lax.div(index, n_tensor), "tensor": lax.rem(index, n_tensor)}

    barrier = pltpu.get_barrier_semaphore()

    @pl.loop(1, n_dev)
    def _(off):
        pl.semaphore_signal(
            barrier, inc=1, device_id=device(lax.rem(me + off, n_dev)), device_id_type=MESH
        )

    pl.semaphore_wait(barrier, n_dev - 1)

    def hop(off):
        peer = lax.rem(tensor + off, n_tensor)
        return pltpu.make_async_remote_copy(
            src_ref=w_ref.at[:, peer],
            dst_ref=owned.at[:, me],
            send_sem=hop_send.at[off],
            recv_sem=hop_recv.at[tensor],
            device_id={"dp": dp, "tensor": peer},
            device_id_type=MESH,
        )

    def hop_arrival(off):
        peer = lax.rem(tensor + off, n_tensor)
        return pltpu.make_async_remote_copy(
            src_ref=w_ref.at[:, peer],
            dst_ref=owned.at[:, dp * n_tensor + peer],
            send_sem=hop_send.at[off],
            recv_sem=hop_recv.at[peer],
            device_id={"dp": dp, "tensor": peer},
            device_id_type=MESH,
        )

    for off in range(1, n_tensor):
        hop(off).start()
    for block in range(tok_tiles.shape[0]):
        tok_tiles[block] = tok_ref[:, block * BLK : (block + 1) * BLK]
        cot_tiles[block] = cot_ref[:, block * BLK : (block + 1) * BLK]
    for mat in range(3):
        owned[mat, me] = w_ref[mat, tensor]

    def pick(src_ref, table, column, dst, slot):
        for k in range(keep):
            dst[slot, table, :, k * BLK : (k + 1) * BLK] = src_ref[kept_ref[table, column, k]]

    def tok_copy(off, table):
        peer = lax.rem(tensor + off, n_tensor)
        return pltpu.make_async_remote_copy(
            src_ref=pack.at[off, table],
            dst_ref=rows.at[tensor, table],
            send_sem=tok_send.at[off, table],
            recv_sem=tok_recv.at[tensor, table],
            device_id={"dp": dp, "tensor": peer},
            device_id_type=MESH,
        )

    def tok_arrival(off, table):
        peer = lax.rem(tensor + off, n_tensor)
        return pltpu.make_async_remote_copy(
            src_ref=pack.at[off, table],
            dst_ref=rows.at[peer, table],
            send_sem=tok_send.at[off, table],
            recv_sem=tok_recv.at[peer, table],
            device_id={"dp": dp, "tensor": peer},
            device_id_type=MESH,
        )

    half = n_tensor // 2
    order = [half] + [o for o in range(1, n_tensor) if o != half]
    for off in order:
        peer = lax.rem(tensor + off, n_tensor)
        for table, src_ref in ((0, tok_tiles), (1, cot_tiles)):
            pick(src_ref, table, peer, pack, off)
            tok_copy(off, table).start()

    for off in range(1, n_tensor):
        hop_arrival(off).wait_recv()

    def ring(off, origin):
        peer = lax.rem(dp + off, n_dp)
        where = owned.at[:, pl.ds(origin * n_tensor, n_tensor)]
        return pltpu.make_async_remote_copy(
            src_ref=where,
            dst_ref=where,
            send_sem=ring_send.at[off],
            recv_sem=ring_recv.at[origin],
            device_id={"dp": peer, "tensor": tensor},
            device_id_type=MESH,
        )

    for off in range(1, n_dp):
        ring(off, dp).start()
    for table, src_ref in ((0, tok_tiles), (1, cot_tiles)):
        pick(src_ref, table, tensor, rows, tensor)
    for off in range(1, n_dp):
        ring(off, lax.rem(dp + off, n_dp)).wait_recv()

    def forward(source):
        x = rows[source, 0]
        y = rows[source, 1]
        mats = [owned[m].reshape(keep * BLK, BLK) for m in range(2)]
        gate = jnp.dot(x, mats[0], preferred_element_type=F32)
        up_val = jnp.dot(x, mats[1], preferred_element_type=F32)
        grad_hidden = jnp.zeros((tok_dev, BLK), F32)
        for k in range(keep):
            grad_hidden += lax.dot_general(
                y[:, k * BLK : (k + 1) * BLK], owned[2, k], (((1,), (1,)), ((), ())),
                preferred_element_type=F32,
            )
        hidden, grad_gate, grad_up = activations(gate, up_val, grad_hidden)
        act[source, :, 0:BLK] = grad_gate
        act[source, :, BLK : 2 * BLK] = grad_up
        act[source, :, 2 * BLK : 3 * BLK] = hidden

    @pl.loop(0, n_tensor)
    def _(off):
        @pl.when(off > 0)
        def _():
            for table in range(2):
                tok_arrival(off, table).wait_recv()

        forward(lax.rem(tensor + off, n_tensor))

    row_count = n_tensor * tok_dev

    def block_grads(index):
        lanes = pl.ds(pl.multiple_of(index * BLK, BLK), BLK)
        x = rows[:, 0, :, lanes].reshape(row_count, BLK)
        y = rows[:, 1, :, lanes].reshape(row_count, BLK)
        first = act[:, :, 0 : 2 * BLK].reshape(row_count, 2 * BLK)
        hidden = act[:, :, 2 * BLK : 3 * BLK].reshape(row_count, BLK)
        both = lax.dot_general(x, first, (((0,), (0,)), ((), ())), preferred_element_type=F32)
        down = lax.dot_general(hidden, y, (((0,), (0,)), ((), ())), preferred_element_type=F32)
        return both[:, :BLK].astype(BF16), both[:, BLK:].astype(BF16), down.astype(BF16)

    def grad_copy(index):
        return pltpu.make_async_remote_copy(
            src_ref=grads.at[index],
            dst_ref=parts.at[me],
            send_sem=grad_send.at[index],
            recv_sem=grad_recv.at[me],
            device_id=device(index),
            device_id_type=MESH,
        )

    def grad_arrival(index):
        return pltpu.make_async_remote_copy(
            src_ref=grads.at[index],
            dst_ref=parts.at[index],
            send_sem=grad_send.at[index],
            recv_sem=grad_recv.at[index],
            device_id=device(index),
            device_id_type=MESH,
        )

    def away(step):
        return lax.rem(me + 1 + lax.rem(step + n_dev // 2 - 1, n_dev - 1), n_dev)

    @pl.loop(0, n_dev - 1)
    def _(step):
        index = away(step)
        for m, block in enumerate(block_grads(index)):
            grads[index, m] = block
        grad_copy(index).start()

    for m, block in enumerate(block_grads(me)):
        parts[me, m] = block

    @pl.loop(0, n_dev - 1)
    def _(step):
        grad_arrival(away(step)).wait_recv()

    for column in range(n_tensor):
        for m in range(3):
            total = parts[column, m].astype(F32)
            for d in range(1, n_dp):
                total += parts[d * n_tensor + column, m].astype(F32)
            out_ref[m, column] = total

    for off in range(1, n_tensor):
        hop(off).wait_send()
        for table in range(2):
            tok_copy(off, table).wait_send()
    for off in range(1, n_dp):
        ring(off, dp).wait_send()

    @pl.loop(0, n_dev - 1)
    def _(step):
        grad_copy(away(step)).wait_send()


def fused(n_dp, n_tensor, tokens, cotangent, weights, kept):
    n_dev = n_dp * n_tensor
    keep = kept.shape[2]
    tok_dev = tokens.shape[0]
    vmem = pl.BlockSpec(memory_space=pltpu.VMEM)
    blocks = weights.reshape(3, n_tensor, BLK, BLK)
    out = pl.pallas_call(
        functools.partial(fused_kernel, n_dp, n_tensor),
        out_shape=jax.ShapeDtypeStruct((3, n_tensor, BLK, BLK), F32),
        in_specs=[pl.BlockSpec(memory_space=pltpu.SMEM), vmem, vmem, vmem],
        out_specs=vmem,
        scratch_shapes=[
            pltpu.VMEM((tokens.shape[1] // BLK, tok_dev, BLK), BF16),
            pltpu.VMEM((tokens.shape[1] // BLK, tok_dev, BLK), BF16),
            pltpu.VMEM((n_tensor, 2, tok_dev, keep * BLK), BF16),
            pltpu.VMEM((n_tensor, 2, tok_dev, keep * BLK), BF16),
            pltpu.VMEM((3, keep, BLK, BLK), BF16),
            pltpu.VMEM((n_tensor, tok_dev, 3 * BLK), BF16),
            pltpu.VMEM((n_dev, 3, BLK, BLK), BF16),
            pltpu.VMEM((n_dev, 3, BLK, BLK), BF16),
            pltpu.SemaphoreType.DMA((n_tensor, 2)),
            pltpu.SemaphoreType.DMA((n_tensor, 2)),
            pltpu.SemaphoreType.DMA((n_tensor,)),
            pltpu.SemaphoreType.DMA((n_tensor,)),
            pltpu.SemaphoreType.DMA((n_dp,)),
            pltpu.SemaphoreType.DMA((n_dp,)),
            pltpu.SemaphoreType.DMA((n_dev,)),
            pltpu.SemaphoreType.DMA((n_dev,)),
        ],
        compiler_params=pltpu.CompilerParams(
            collective_id=0, has_side_effects=True, vmem_limit_bytes=48 * 1024 * 1024
        ),
    )(kept, tokens, cotangent, blocks)
    return out.reshape(3, n_tensor, BLK * BLK)


def staged(tokens, cotangent, weights, kept):
    tok_rows, cot_rows = (
        lax.all_gather(tokens, "tensor", axis=0, tiled=True),
        lax.all_gather(cotangent, "tensor", axis=0, tiled=True),
    )
    tensor_size = lax.axis_size("tensor")
    dp_size = lax.axis_size("dp")
    tensor_rank = lax.axis_index("tensor")
    columns = weights.shape[1]
    cols_dev = columns // tensor_size
    slice_len = weights.shape[2]
    gathered = lax.all_gather(weights, "dp", axis=2, tiled=True)
    owned = lax.all_to_all(gathered, "tensor", split_axis=1, concat_axis=2, tiled=True)
    owned = owned.reshape(3, cols_dev, tensor_size, dp_size, slice_len)
    owned = jnp.transpose(owned, (0, 1, 3, 2, 4))
    blocks = owned.reshape(3, cols_dev, -1, BLK, BLK)
    tables = lax.dynamic_slice_in_dim(kept, tensor_rank * cols_dev, cols_dev, 1)
    row_count = tok_rows.shape[0]
    picked_x = jnp.take(tok_rows.reshape(row_count, -1, BLK), tables[0], axis=1)
    picked_y = jnp.take(cot_rows.reshape(row_count, -1, BLK), tables[1], axis=1)
    gate = jnp.einsum("rckb,ckbs->rcs", picked_x, blocks[0], preferred_element_type=F32)
    up_val = jnp.einsum("rckb,ckbs->rcs", picked_x, blocks[1], preferred_element_type=F32)
    grad_hidden = jnp.einsum("rcks,ckhs->rch", picked_y, blocks[2], preferred_element_type=F32)
    hidden, grad_gate, grad_up = activations(gate, up_val, grad_hidden)
    gate_grad = jnp.einsum("rckb,rcs->ckbs", picked_x, grad_gate, preferred_element_type=F32)
    up_grad = jnp.einsum("rckb,rcs->ckbs", picked_x, grad_up, preferred_element_type=F32)
    down_grad = jnp.einsum("rch,rcks->ckhs", hidden, picked_y, preferred_element_type=F32)
    partial_grads = jnp.stack([gate_grad, up_grad, down_grad]).reshape(3, cols_dev, -1)
    summed = lax.psum_scatter(partial_grads, "dp", scatter_dimension=2, tiled=True)
    return lax.all_to_all(summed, "tensor", split_axis=2, concat_axis=1, tiled=True)


def solution(mesh):
    n_dp, n_tensor = mesh.shape["dp"], mesh.shape["tensor"]

    def per_device(tokens, cotangent, weights, kept):
        if weights.shape[1] == n_tensor and weights.shape[2] == BLK * BLK:
            return fused(n_dp, n_tensor, tokens, cotangent, weights, kept)
        return staged(tokens, cotangent, weights, kept)

    in_specs = (
        P(("group", "dp", "tensor"), None),
        P(("group", "dp", "tensor"), None),
        P(None, None, ("dp", "tensor")),
        P(),
    )
    out_specs = P("group", None, ("dp", "tensor"))
    return jax.shard_map(
        per_device, mesh=mesh, in_specs=in_specs, out_specs=out_specs, check_vma=False
    )
```

time: 798 us -> 100 us (0.13); the launches traced: 784 us -> 100 us
  other arithmetic: 301 us -> 0 us
  waiting for transfers between devices: 228 us -> 0 us
  local copies, waits for them, and re-layouts: 214 us -> 5.09 us
  Pallas kernels: 0 us -> 94.8 us
  blocking collectives: 14.2 us -> 0 us
  between operations: 14.2 us -> 0.03 us
  matrix products: 9.92 us -> 0 us
    unnamed x1 -> x0, other arithmetic: 291 us -> none
    unnamed x5 -> x0, waiting for transfers between devices: 119 us -> none
    unnamed x22 -> x6, local copies, waits for them, and re-layouts: 117 us -> 2.45 us
    pallas_call x0 -> x1, Pallas kernels: none -> 94.8 us  [fused(): pl.pallas_call(functools.partial(fused_kernel, n_dp, n_tensor), out_shape...]
    all_gather x3 -> x0, waiting for transfers between devices: 64.3 us -> none  [the longest x1 46 us: per_device(): gathered = lax.all_gather(weights, 'dp', axis=2, tiled=True)]
    reduce_scatter x1 -> x0, local copies, waits for them, and re-layouts: 47.6 us -> none  [per_device(): lax.psum_scatter(partial_grads, 'dp', scatter_dimension=2, tiled=True)]
    all_to_all x1 -> x0, waiting for transfers between devices: 43.8 us -> none  [per_device(): lax.all_to_all(gathered, 'tensor', split_axis=1, concat_axis=2, tiled=True)]
    all_to_all x1 -> x0, local copies, waits for them, and re-layouts: 18.2 us -> none  [per_device(): lax.all_to_all(summed, 'tensor', split_axis=2, concat_axis=1, tiled=True)]
  transfers between devices with their start and end apart: 5 -> 0, of which waited for: 4 -> 0; matrix products, arithmetic and copies ran while one was open for 3% -> 0% of each run, Pallas kernels for 0% -> 0%
where the time goes in v1:
time: 100 us
  Pallas kernels  94.8 us (95%)
  local copies, waits for them, and re-layouts  5.09 us (5%)
    pallas_call x1, Pallas kernels, fused(): pl.pallas_call(functools.partial(fused_kernel, n_dp, n_tensor), out_shape...  94.8 us
    unnamed x6, local copies, waits for them, and re-layouts  2.45 us

profile of v1, /device:TPU:0, one launch (start us, length us, event | category | flops | bytes accessed | tf_op | source)
XLA Modules:
  0.0 100.0 jit_solution(3185336647205745519)
XLA Ops:
  0.0 0.0 copy-start.2
  0.0 1.4 %reshape.6.w_ref = bf16[3,4,128,128]{3,2,1,0:T(8,128)(2,1)S(1)} reshape(bf16[3,4,16384]{2,1,0:T(4,128)(2,1)} %param.6) | data formatting | bytes 786432 | tf_op jit(solution)/shard_map/reshape | solution.py:236
  1.4 0.0 copy-done.2
  1.4 0.0 copy-start
  1.4 1.2 %copy-done = bf16[128,4096]{1,0:T(8,128)(2,1)S(1)} copy-done((bf16[128,4096]{1,0:T(8,128)(2,1)S(1)}, bf16[128,4096]{1,0:T(8,128)(2,1)}, u32[]{:S(2)}) %copy-start) | copy-done | bytes 1048600
  2.7 0.0 copy-start.1
  2.7 1.2 %copy-done.1 = bf16[128,4096]{1,0:T(8,128)(2,1)S(1)} copy-done((bf16[128,4096]{1,0:T(8,128)(2,1)S(1)}, bf16[128,4096]{1,0:T(8,128)(2,1)}, u32[]{:S(2)}) %copy-start.1) | copy-done | bytes 1048600
  3.9 94.8 %shard_map.46 = f32[3,4,128,128]{3,2,1,0:T(8,128)S(1)} custom-call(s32[2,4,16]{2,1,0:T(4,128)S(1)} %copy-done.2, bf16[128,4096]{1,0:T(8,128)(2,1)S(1)} %copy-done, bf16[128,4096]{1,0:T(8,128)(2,1)S(1)} %copy-done.1, bf16[3,4,128,128]{3,2,1,0:T(8,128)(2,1)S(1)} %reshape.6.w_ref), custom_call_target="tpu_custom_call" | custom-call | tf_op jit(solution)/shard_map/pallas_call | solution.py:237
  98.7 1.2 %reshape.7 = f32[3,4,16384]{2,1,0:T(4,128)} reshape(f32[3,4,128,128]{3,2,1,0:T(8,128)S(1)} %shard_map.46) | data formatting | bytes 1572864 | tf_op jit(solution)/shard_map/reshape | solution.py:264
Async XLA Ops:
  0.0 1.4 %copy-start.2 = (s32[2,4,16]{2,1,0:T(4,128)S(1)}, s32[2,4,16]{2,1,0:T(4,128)}, u32[]{:S(2)}) copy-start(s32[2,4,16]{2,1,0:T(4,128)} %kept_ref.1) | copy-start | bytes 1540
  1.4 1.2 %copy-start = (bf16[128,4096]{1,0:T(8,128)(2,1)S(1)}, bf16[128,4096]{1,0:T(8,128)(2,1)}, u32[]{:S(2)}) copy-start(bf16[128,4096]{1,0:T(8,128)(2,1)} %tok_ref.1) | copy-start | bytes 3145732
  2.7 1.2 %copy-start.1 = (bf16[128,4096]{1,0:T(8,128)(2,1)S(1)}, bf16[128,4096]{1,0:T(8,128)(2,1)}, u32[]{:S(2)}) copy-start(bf16[128,4096]{1,0:T(8,128)(2,1)} %cot_ref.1) | copy-start | bytes 3145732

commit v2 on v0

v2 whole, which is shorter than its diff:
```python
import functools

import jax
import jax.numpy as jnp
from jax import lax
from jax.experimental import pallas as pl
from jax.experimental.pallas import tpu as pltpu
from jax.sharding import PartitionSpec as P

BLK = 128
MESH = pl.DeviceIdType.MESH
F32 = jnp.float32
BF16 = jnp.bfloat16


def activations(gate, up_val, grad_hidden):
    sigmoid_gate = jax.nn.sigmoid(gate)
    silu_gate = gate * sigmoid_gate
    hidden = (silu_gate * up_val).astype(BF16)
    grad_gate = (grad_hidden * up_val * sigmoid_gate * (1.0 + gate * (1.0 - sigmoid_gate))).astype(BF16)
    grad_up = (grad_hidden * silu_gate).astype(BF16)
    return hidden, grad_gate, grad_up


def fused_kernel(
    n_dp, n_tensor,
    kept_ref, tok_ref, cot_ref, w_ref, out_ref,
    x_mine, y_mine, x_mate, y_mate, stage, owned, x_rows, x_cols, y_rows, y_blocks,
    act, hid, pair_out, pair_in, home_out, parts,
    mate_send, mate_recv, near_send, cross_send, own_recv,
    pair_send, pair_recv, home_send, home_recv,
):
    cores = 2
    cols = n_tensor // cores
    peers = n_dp * cores
    keep = kept_ref.shape[2]
    tok_dev = tok_ref.shape[0]
    dp = lax.axis_index("dp")
    tensor = lax.axis_index("tensor")
    chip = lax.div(tensor, cores)
    core = lax.rem(tensor, cores)
    far = 1 - chip
    mine = dp * cores + core
    mate = dp * cores + 1 - core

    def near(i):
        return {"dp": lax.div(i, cores), "tensor": chip * cores + lax.rem(i, cores)}

    partner = {"dp": dp, "tensor": far * cores + core}
    barrier = pltpu.get_barrier_semaphore()

    @pl.loop(1, peers)
    def _(off):
        pl.semaphore_signal(
            barrier, inc=1, device_id=near(lax.rem(mine + off, peers)), device_id_type=MESH
        )

    pl.semaphore_signal(barrier, inc=1, device_id=partner, device_id_type=MESH)

    for column in range(n_tensor):
        for m in range(3):
            stage[column, :, m * BLK : (m + 1) * BLK] = w_ref[m, column]
    for a in range(cols):
        owned[a, chip, mine] = stage[core * cols + a]

    pl.semaphore_wait(barrier, peers)

    def near_copy(a, off):
        i = lax.rem(mine + off, peers)
        return pltpu.make_async_remote_copy(
            src_ref=stage.at[lax.rem(i, cores) * cols + a],
            dst_ref=owned.at[a, chip, mine],
            send_sem=near_send.at[a, off],
            recv_sem=own_recv.at[a, chip, mine],
            device_id=near(i),
            device_id_type=MESH,
        )

    def cross_copy(a, side, i):
        return pltpu.make_async_remote_copy(
            src_ref=owned.at[a, side, i],
            dst_ref=owned.at[a, side, i],
            send_sem=cross_send.at[a, i],
            recv_sem=own_recv.at[a, side, i],
            device_id=partner,
            device_id_type=MESH,
        )

    for a in range(cols):
        cross_copy(a, chip, mine).start()
        for off in range(1, peers):
            near_copy(a, off).start()

    def mate_copy(table):
        return pltpu.make_async_remote_copy(
            src_ref=(x_mine, y_mine)[table],
            dst_ref=(x_mate, y_mate)[table],
            send_sem=mate_send.at[table],
            recv_sem=mate_recv.at[table],
            device_id=near(mate),
            device_id_type=MESH,
        )

    for table, (src_ref, tiles) in enumerate(((tok_ref, x_mine), (cot_ref, y_mine))):
        for block in range(tiles.shape[0]):
            tiles[block] = src_ref[:, block * BLK : (block + 1) * BLK]
        mate_copy(table).start()

    def relay(a, i):
        copy = cross_copy(a, chip, i)
        copy.wait_recv()
        copy.start()

    for a in range(cols):
        relay(a, mate)
    for table in range(2):
        mate_copy(table).wait_recv()

    def pack(a):
        for side in range(n_tensor // cores):
            for i in range(peers):
                k = (i // cores) * n_tensor + side * cores + i % cores
                p = side * peers + i
                lanes = slice(p * BLK, (p + 1) * BLK)
                column = core * cols + a
                index = kept_ref[0, column, k]
                block = jnp.concatenate([x_mine[index], x_mate[index]], axis=0)
                x_rows[a, :, lanes] = block
                x_cols[a, side, i] = block.T
                index = kept_ref[1, column, k]
                block = jnp.concatenate([y_mine[index], y_mate[index]], axis=0)
                y_rows[a, :, lanes] = block
                y_blocks[a, side, i] = block

    def later(step):
        return lax.rem(mine - core + cores + step, peers)

    def forward(a):
        both = jnp.dot(
            x_rows[a], owned[a, :, :, :, 0 : 2 * BLK].reshape(keep * BLK, 2 * BLK),
            preferred_element_type=F32,
        )
        grad_hidden = jnp.zeros((cores * tok_dev, BLK), F32)
        for p in range(0, keep, 2):
            side, i = divmod(p, peers)
            down = jnp.concatenate(
                [owned[a, side, i, :, 2 * BLK :], owned[a, side, i + 1, :, 2 * BLK :]], axis=1
            )
            grad_hidden += lax.dot_general(
                y_rows[a, :, p * BLK : (p + 2) * BLK], down, (((1,), (1,)), ((), ())),
                preferred_element_type=F32,
            )
        hidden, grad_gate, grad_up = activations(both[:, :BLK], both[:, BLK:], grad_hidden)
        act[a, :, 0:BLK] = grad_gate
        act[a, :, BLK : 2 * BLK] = grad_up
        hid[a] = hidden.T

    def block_grads(a, side, i):
        both = jnp.dot(x_cols[a, side, i], act[a], preferred_element_type=F32)
        down = jnp.dot(hid[a], y_blocks[a, side, i], preferred_element_type=F32)
        return jnp.concatenate([both, down], axis=1)

    def pair_copy(a, i):
        return pltpu.make_async_remote_copy(
            src_ref=pair_out.at[a, i],
            dst_ref=pair_in.at[a, i],
            send_sem=pair_send.at[a, i],
            recv_sem=pair_recv.at[a, i],
            device_id=partner,
            device_id_type=MESH,
        )

    def home_copy(a, i):
        return pltpu.make_async_remote_copy(
            src_ref=home_out.at[a, i],
            dst_ref=parts.at[core * cols + a, dp],
            send_sem=home_send.at[a, i],
            recv_sem=home_recv.at[core * cols + a, dp],
            device_id=near(i),
            device_id_type=MESH,
        )

    def to_pair(a, step):
        i = lax.rem(mine + peers // 2 + step, peers)
        pair_out[a, i] = block_grads(a, far, i).astype(BF16)
        pair_copy(a, i).start()

    def to_home(a, step):
        i = lax.rem(mine + peers // 2 + step, peers)
        pair_copy(a, i).wait_recv()
        total = (block_grads(a, chip, i) + pair_in[a, i].astype(F32)).astype(BF16)

        @pl.when(i == mine)
        def _():
            parts[core * cols + a, dp] = total

        @pl.when(i != mine)
        def _():
            home_out[a, i] = total
            home_copy(a, i).start()

    def crossed(a):
        @pl.loop(0, peers)
        def _(i):
            cross_copy(a, far, i).wait_recv()

    pack(0)

    @pl.loop(0, peers - cores)
    def _(step):
        relay(0, later(step))

    pack(1)
    crossed(0)
    forward(0)

    @pl.loop(0, peers)
    def _(step):
        @pl.when(step < peers - cores)
        def _():
            relay(1, later(step))

        to_pair(0, step)

    crossed(1)
    forward(1)

    @pl.loop(0, peers)
    def _(step):
        to_pair(1, step)
        to_home(0, step)

    @pl.loop(0, peers)
    def _(step):
        to_home(1, step)

    for column in range(n_tensor):
        for d in range(n_dp):
            @pl.when(jnp.logical_or(core != column // cols, dp != d))
            def _():
                pltpu.make_async_remote_copy(
                    src_ref=home_out.at[0, 0],
                    dst_ref=parts.at[column, d],
                    send_sem=home_send.at[0, 0],
                    recv_sem=home_recv.at[column, d],
                    device_id=near(mate),
                    device_id_type=MESH,
                ).wait_recv()

        total = parts[column, 0].astype(F32)
        for d in range(1, n_dp):
            total += parts[column, d].astype(F32)
        for m in range(3):
            out_ref[m, column] = total[:, m * BLK : (m + 1) * BLK]

    for table in range(2):
        mate_copy(table).wait_send()
    for a in range(cols):
        for off in range(1, peers):
            near_copy(a, off).wait_send()

        @pl.loop(0, peers)
        def _(i):
            cross_copy(a, chip, i).wait_send()
            pair_copy(a, i).wait_send()

            @pl.when(i != mine)
            def _():
                home_copy(a, i).wait_send()


def fused(n_dp, n_tensor, tokens, cotangent, weights, kept):
    cores, chips = 2, n_tensor // 2
    cols = n_tensor // cores
    peers = n_dp * cores
    keep = kept.shape[2]
    tok_dev = tokens.shape[0]
    tiles = tokens.shape[1] // BLK
    rows = cores * tok_dev
    vmem = pl.BlockSpec(memory_space=pltpu.VMEM)
    blocks = weights.reshape(3, n_tensor, BLK, BLK)
    dma = pltpu.SemaphoreType.DMA
    out = pl.pallas_call(
        functools.partial(fused_kernel, n_dp, n_tensor),
        out_shape=jax.ShapeDtypeStruct((3, n_tensor, BLK, BLK), F32),
        in_specs=[pl.BlockSpec(memory_space=pltpu.SMEM), vmem, vmem, vmem],
        out_specs=vmem,
        scratch_shapes=[
            pltpu.VMEM((tiles, tok_dev, BLK), BF16),
            pltpu.VMEM((tiles, tok_dev, BLK), BF16),
            pltpu.VMEM((tiles, tok_dev, BLK), BF16),
            pltpu.VMEM((tiles, tok_dev, BLK), BF16),
            pltpu.VMEM((n_tensor, BLK, 3 * BLK), BF16),
            pltpu.VMEM((cols, chips, peers, BLK, 3 * BLK), BF16),
            pltpu.VMEM((cols, rows, keep * BLK), BF16),
            pltpu.VMEM((cols, chips, peers, BLK, rows), BF16),
            pltpu.VMEM((cols, rows, keep * BLK), BF16),
            pltpu.VMEM((cols, chips, peers, rows, BLK), BF16),
            pltpu.VMEM((cols, rows, 2 * BLK), BF16),
            pltpu.VMEM((cols, BLK, rows), BF16),
            pltpu.VMEM((cols, peers, BLK, 3 * BLK), BF16),
            pltpu.VMEM((cols, peers, BLK, 3 * BLK), BF16),
            pltpu.VMEM((cols, peers, BLK, 3 * BLK), BF16),
            pltpu.VMEM((n_tensor, n_dp, BLK, 3 * BLK), BF16),
            dma((2,)),
            dma((2,)),
            dma((cols, peers)),
            dma((cols, peers)),
            dma((cols, chips, peers)),
            dma((cols, peers)),
            dma((cols, peers)),
            dma((cols, peers)),
            dma((n_tensor, n_dp)),
        ],
        compiler_params=pltpu.CompilerParams(
            collective_id=0, has_side_effects=True, vmem_limit_bytes=48 * 1024 * 1024
        ),
    )(kept, tokens, cotangent, blocks)
    return out.reshape(3, n_tensor, BLK * BLK)


def staged(tokens, cotangent, weights, kept):
    tok_rows, cot_rows = (
        lax.all_gather(tokens, "tensor", axis=0, tiled=True),
        lax.all_gather(cotangent, "tensor", axis=0, tiled=True),
    )
    tensor_size = lax.axis_size("tensor")
    dp_size = lax.axis_size("dp")
    tensor_rank = lax.axis_index("tensor")
    columns = weights.shape[1]
    cols_dev = columns // tensor_size
    slice_len = weights.shape[2]
    gathered = lax.all_gather(weights, "dp", axis=2, tiled=True)
    owned = lax.all_to_all(gathered, "tensor", split_axis=1, concat_axis=2, tiled=True)
    owned = owned.reshape(3, cols_dev, tensor_size, dp_size, slice_len)
    owned = jnp.transpose(owned, (0, 1, 3, 2, 4))
    blocks = owned.reshape(3, cols_dev, -1, BLK, BLK)
    tables = lax.dynamic_slice_in_dim(kept, tensor_rank * cols_dev, cols_dev, 1)
    row_count = tok_rows.shape[0]
    picked_x = jnp.take(tok_rows.reshape(row_count, -1, BLK), tables[0], axis=1)
    picked_y = jnp.take(cot_rows.reshape(row_count, -1, BLK), tables[1], axis=1)
    gate = jnp.einsum("rckb,ckbs->rcs", picked_x, blocks[0], preferred_element_type=F32)
    up_val = jnp.einsum("rckb,ckbs->rcs", picked_x, blocks[1], preferred_element_type=F32)
    grad_hidden = jnp.einsum("rcks,ckhs->rch", picked_y, blocks[2], preferred_element_type=F32)
    hidden, grad_gate, grad_up = activations(gate, up_val, grad_hidden)
    gate_grad = jnp.einsum("rckb,rcs->ckbs", picked_x, grad_gate, preferred_element_type=F32)
    up_grad = jnp.einsum("rckb,rcs->ckbs", picked_x, grad_up, preferred_element_type=F32)
    down_grad = jnp.einsum("rch,rcks->ckhs", hidden, picked_y, preferred_element_type=F32)
    partial_grads = jnp.stack([gate_grad, up_grad, down_grad]).reshape(3, cols_dev, -1)
    summed = lax.psum_scatter(partial_grads, "dp", scatter_dimension=2, tiled=True)
    return lax.all_to_all(summed, "tensor", split_axis=2, concat_axis=1, tiled=True)


def solution(mesh):
    n_dp, n_tensor = mesh.shape["dp"], mesh.shape["tensor"]

    def per_device(tokens, cotangent, weights, kept):
        if weights.shape[1] == n_tensor == 4 and weights.shape[2] == BLK * BLK:
            return fused(n_dp, n_tensor, tokens, cotangent, weights, kept)
        return staged(tokens, cotangent, weights, kept)

    in_specs = (
        P(("group", "dp", "tensor"), None),
        P(("group", "dp", "tensor"), None),
        P(None, None, ("dp", "tensor")),
        P(),
    )
    out_specs = P("group", None, ("dp", "tensor"))
    return jax.shard_map(
        per_device, mesh=mesh, in_specs=in_specs, out_specs=out_specs, check_vma=False
    )
```

time: 798 us -> 103 us (0.13); the launches traced: 784 us -> 102 us
  other arithmetic: 301 us -> 0 us
  waiting for transfers between devices: 228 us -> 0 us
  local copies, waits for them, and re-layouts: 214 us -> 5.09 us
  Pallas kernels: 0 us -> 96.9 us
  blocking collectives: 14.2 us -> 0 us
  between operations: 14.2 us -> 0.03 us
  matrix products: 9.92 us -> 0 us
    unnamed x1 -> x0, other arithmetic: 291 us -> none
    unnamed x5 -> x0, waiting for transfers between devices: 119 us -> none
    unnamed x22 -> x6, local copies, waits for them, and re-layouts: 117 us -> 2.45 us
    pallas_call x0 -> x1, Pallas kernels: none -> 96.9 us  [fused(): pl.pallas_call(functools.partial(fused_kernel, n_dp, n_tensor), out_shape...]
    all_gather x3 -> x0, waiting for transfers between devices: 64.3 us -> none  [the longest x1 46 us: per_device(): gathered = lax.all_gather(weights, 'dp', axis=2, tiled=True)]
    reduce_scatter x1 -> x0, local copies, waits for them, and re-layouts: 47.6 us -> none  [per_device(): lax.psum_scatter(partial_grads, 'dp', scatter_dimension=2, tiled=True)]
    all_to_all x1 -> x0, waiting for transfers between devices: 43.8 us -> none  [per_device(): lax.all_to_all(gathered, 'tensor', split_axis=1, concat_axis=2, tiled=True)]
    all_to_all x1 -> x0, local copies, waits for them, and re-layouts: 18.2 us -> none  [per_device(): lax.all_to_all(summed, 'tensor', split_axis=2, concat_axis=1, tiled=True)]
  transfers between devices with their start and end apart: 5 -> 0, of which waited for: 4 -> 0; matrix products, arithmetic and copies ran while one was open for 3% -> 0% of each run, Pallas kernels for 0% -> 0%
where the time goes in v2:
time: 103 us; the launch traced here: 102 us
  Pallas kernels  96.9 us (94%)
  local copies, waits for them, and re-layouts  5.09 us (5%)
    pallas_call x1, Pallas kernels, fused(): pl.pallas_call(functools.partial(fused_kernel, n_dp, n_tensor), out_shape...  96.9 us
    unnamed x6, local copies, waits for them, and re-layouts  2.45 us

profile of v2, /device:TPU:0, one launch (start us, length us, event | category | flops | bytes accessed | tf_op | source)
XLA Modules:
  0.0 102.0 jit_solution(16126078831806712272)
XLA Ops:
  0.0 0.0 copy-start.2
  0.0 1.4 %reshape.6.w_ref = bf16[3,4,128,128]{3,2,1,0:T(8,128)(2,1)S(1)} reshape(bf16[3,4,16384]{2,1,0:T(4,128)(2,1)} %param.6) | data formatting | bytes 786432 | tf_op jit(solution)/shard_map/reshape | solution.py:281
  1.4 0.0 copy-done.2
  1.4 0.0 copy-start
  1.4 1.2 %copy-done = bf16[128,4096]{1,0:T(8,128)(2,1)S(1)} copy-done((bf16[128,4096]{1,0:T(8,128)(2,1)S(1)}, bf16[128,4096]{1,0:T(8,128)(2,1)}, u32[]{:S(2)}) %copy-start) | copy-done | bytes 1048600
  2.7 0.0 copy-start.1
  2.7 1.2 %copy-done.1 = bf16[128,4096]{1,0:T(8,128)(2,1)S(1)} copy-done((bf16[128,4096]{1,0:T(8,128)(2,1)S(1)}, bf16[128,4096]{1,0:T(8,128)(2,1)}, u32[]{:S(2)}) %copy-start.1) | copy-done | bytes 1048600
  3.9 96.9 %shard_map.46 = f32[3,4,128,128]{3,2,1,0:T(8,128)S(1)} custom-call(s32[2,4,16]{2,1,0:T(4,128)S(1)} %copy-done.2, bf16[128,4096]{1,0:T(8,128)(2,1)S(1)} %copy-done, bf16[128,4096]{1,0:T(8,128)(2,1)S(1)} %copy-done.1, bf16[3,4,128,128]{3,2,1,0:T(8,128)(2,1)S(1)} %reshape.6.w_ref), custom_call_target="tpu_custom_call" | custom-call | tf_op jit(solution)/shard_map/pallas_call | solution.py:283
  100.8 1.2 %reshape.7 = f32[3,4,16384]{2,1,0:T(4,128)} reshape(f32[3,4,128,128]{3,2,1,0:T(8,128)S(1)} %shard_map.46) | data formatting | bytes 1572864 | tf_op jit(solution)/shard_map/reshape | solution.py:319
Async XLA Ops:
  0.0 1.4 %copy-start.2 = (s32[2,4,16]{2,1,0:T(4,128)S(1)}, s32[2,4,16]{2,1,0:T(4,128)}, u32[]{:S(2)}) copy-start(s32[2,4,16]{2,1,0:T(4,128)} %kept_ref.1) | copy-start | bytes 1540
  1.4 1.2 %copy-start = (bf16[128,4096]{1,0:T(8,128)(2,1)S(1)}, bf16[128,4096]{1,0:T(8,128)(2,1)}, u32[]{:S(2)}) copy-start(bf16[128,4096]{1,0:T(8,128)(2,1)} %tok_ref.1) | copy-start | bytes 3145732
  2.7 1.2 %copy-start.1 = (bf16[128,4096]{1,0:T(8,128)(2,1)S(1)}, bf16[128,4096]{1,0:T(8,128)(2,1)}, u32[]{:S(2)}) copy-start(bf16[128,4096]{1,0:T(8,128)(2,1)} %cot_ref.1) | copy-start | bytes 3145732

commit v3 on v2

--- a/solution.py
+++ b/solution.py
@@ -25,9 +25,9 @@
 def fused_kernel(
     n_dp, n_tensor,
     kept_ref, tok_ref, cot_ref, w_ref, out_ref,
-    x_mine, y_mine, x_mate, y_mate, stage, owned, x_rows, x_cols, y_rows, y_blocks,
+    x_raw, y_raw, x_mine, y_mine, x_mate, y_mate, stage, owned, x_rows, x_cols, y_rows, y_blocks,
     act, hid, pair_out, pair_in, home_out, parts,
-    mate_send, mate_recv, near_send, cross_send, own_recv,
+    fetch, mate_send, mate_recv, shard_send, line_send, cross_send, own_recv,
     pair_send, pair_recv, home_send, home_recv,
 ):
     cores = 2
@@ -49,6 +49,14 @@
     partner = {"dp": dp, "tensor": far * cores + core}
     barrier = pltpu.get_barrier_semaphore()
 
+    def fetch_copy(table):
+        return pltpu.make_async_copy(
+            (tok_ref, cot_ref)[table], (x_raw, y_raw)[table], fetch.at[table]
+        )
+
+    for table in range(2):
+        fetch_copy(table).start()
+
     @pl.loop(1, peers)
     def _(off):
         pl.semaphore_signal(
@@ -65,16 +73,33 @@
 
     pl.semaphore_wait(barrier, peers)
 
-    def near_copy(a, off):
-        i = lax.rem(mine + off, peers)
-        return pltpu.make_async_remote_copy(
-            src_ref=stage.at[lax.rem(i, cores) * cols + a],
+    def shard_copy(a):
+        return pltpu.make_async_remote_copy(
+            src_ref=stage.at[(1 - core) * cols + a],
             dst_ref=owned.at[a, chip, mine],
-            send_sem=near_send.at[a, off],
+            send_sem=shard_send.at[a],
             recv_sem=own_recv.at[a, chip, mine],
-            device_id=near(i),
-            device_id_type=MESH,
-        )
+            device_id=near(mate),
+            device_id_type=MESH,
+        )
+
+    def line_copy(a, way, i):
+        return pltpu.make_async_remote_copy(
+            src_ref=owned.at[a, chip, i],
+            dst_ref=owned.at[a, chip, i],
+            send_sem=line_send.at[a, way, i],
+            recv_sem=own_recv.at[a, chip, i],
+            device_id={"dp": dp + 2 * way - 1, "tensor": tensor},
+            device_id_type=MESH,
+        )
+
+    ends = (dp > 0, dp < n_dp - 1)
+
+    def both_ways(a, i):
+        for way in range(2):
+            @pl.when(ends[way])
+            def _():
+                line_copy(a, way, i).start()
 
     def cross_copy(a, side, i):
         return pltpu.make_async_remote_copy(
@@ -87,9 +112,9 @@
         )
 
     for a in range(cols):
+        shard_copy(a).start()
+        both_ways(a, mine)
         cross_copy(a, chip, mine).start()
-        for off in range(1, peers):
-            near_copy(a, off).start()
 
     def mate_copy(table):
         return pltpu.make_async_remote_copy(
@@ -101,18 +126,33 @@
             device_id_type=MESH,
         )
 
-    for table, (src_ref, tiles) in enumerate(((tok_ref, x_mine), (cot_ref, y_mine))):
+    for table, (src_ref, tiles) in enumerate(((x_raw, x_mine), (y_raw, y_mine))):
+        fetch_copy(table).wait()
         for block in range(tiles.shape[0]):
             tiles[block] = src_ref[:, block * BLK : (block + 1) * BLK]
         mate_copy(table).start()
 
-    def relay(a, i):
-        copy = cross_copy(a, chip, i)
-        copy.wait_recv()
-        copy.start()
-
     for a in range(cols):
-        relay(a, mate)
+        cross_copy(a, chip, mate).wait_recv()
+        both_ways(a, mate)
+        cross_copy(a, chip, mate).start()
+
+    def relay(a, step):
+        hop = 1 + step // cores
+        for way in range(2):
+            other = dp + hop if way == 0 else dp - hop
+
+            @pl.when((other < n_dp) if way == 0 else (other >= 0))
+            def _():
+                i = other * cores + lax.rem(step, cores)
+                copy = cross_copy(a, chip, i)
+                copy.wait_recv()
+
+                @pl.when(ends[way])
+                def _():
+                    line_copy(a, way, i).start()
+
+                copy.start()
     for table in range(2):
         mate_copy(table).wait_recv()
 
@@ -132,9 +172,6 @@
                 y_rows[a, :, lanes] = block
                 y_blocks[a, side, i] = block
 
-    def later(step):
-        return lax.rem(mine - core + cores + step, peers)
-
     def forward(a):
         both = jnp.dot(
             x_rows[a], owned[a, :, :, :, 0 : 2 * BLK].reshape(keep * BLK, 2 * BLK),
@@ -208,7 +245,7 @@
 
     @pl.loop(0, peers - cores)
     def _(step):
-        relay(0, later(step))
+        relay(0, step)
 
     pack(1)
     crossed(0)
@@ -218,7 +255,7 @@
     def _(step):
         @pl.when(step < peers - cores)
         def _():
-            relay(1, later(step))
+            relay(1, step)
 
         to_pair(0, step)
 
@@ -256,13 +293,21 @@
     for table in range(2):
         mate_copy(table).wait_send()
     for a in range(cols):
-        for off in range(1, peers):
-            near_copy(a, off).wait_send()
+        shard_copy(a).wait_send()
 
         @pl.loop(0, peers)
         def _(i):
             cross_copy(a, chip, i).wait_send()
             pair_copy(a, i).wait_send()
+            source = lax.div(i, cores)
+
+            @pl.when(jnp.logical_and(dp > 0, source >= dp))
+            def _():
+                line_copy(a, 0, i).wait_send()
+
+            @pl.when(jnp.logical_and(dp < n_dp - 1, source <= dp))
+            def _():
+                line_copy(a, 1, i).wait_send()
 
             @pl.when(i != mine)
             def _():
@@ -278,14 +323,17 @@
     tiles = tokens.shape[1] // BLK
     rows = cores * tok_dev
     vmem = pl.BlockSpec(memory_space=pltpu.VMEM)
+    hbm = pl.BlockSpec(memory_space=pl.ANY)
     blocks = weights.reshape(3, n_tensor, BLK, BLK)
     dma = pltpu.SemaphoreType.DMA
     out = pl.pallas_call(
         functools.partial(fused_kernel, n_dp, n_tensor),
         out_shape=jax.ShapeDtypeStruct((3, n_tensor, BLK, BLK), F32),
-        in_specs=[pl.BlockSpec(memory_space=pltpu.SMEM), vmem, vmem, vmem],
+        in_specs=[pl.BlockSpec(memory_space=pltpu.SMEM), hbm, hbm, vmem],
         out_specs=vmem,
         scratch_shapes=[
+            pltpu.VMEM(tokens.shape, BF16),
+            pltpu.VMEM(tokens.shape, BF16),
             pltpu.VMEM((tiles, tok_dev, BLK), BF16),
             pltpu.VMEM((tiles, tok_dev, BLK), BF16),
             pltpu.VMEM((tiles, tok_dev, BLK), BF16),
@@ -304,7 +352,9 @@
             pltpu.VMEM((n_tensor, n_dp, BLK, 3 * BLK), BF16),
             dma((2,)),
             dma((2,)),
-            dma((cols, peers)),
+            dma((2,)),
+            dma((cols,)),
+            dma((cols, 2, peers)),
             dma((cols, peers)),
             dma((cols, chips, peers)),
             dma((cols, peers)),

time: 103 us -> 92.7 us (0.900)
  Pallas kernels: 96.9 us -> 87.4 us
    pallas_call x1, Pallas kernels: 96.9 us -> 87.4 us  [fused(): pl.pallas_call(functools.partial(fused_kernel, n_dp, n_tensor), out_shape...]
where the time goes in v3:
time: 92.7 us; the launch traced here: 92.5 us
  Pallas kernels  87.4 us (94%)
  local copies, waits for them, and re-layouts  5.09 us (5%)
    pallas_call x1, Pallas kernels, fused(): pl.pallas_call(functools.partial(fused_kernel, n_dp, n_tensor), out_shape...  87.4 us
    unnamed x6, local copies, waits for them, and re-layouts  2.45 us

profile of v3, /device:TPU:0, one launch (start us, length us, event | category | flops | bytes accessed | tf_op | source)
XLA Modules:
  0.0 92.5 jit_solution(1807415713661660597)
XLA Ops:
  0.0 0.0 copy-start.2
  0.0 1.4 %reshape.6.w_ref = bf16[3,4,128,128]{3,2,1,0:T(8,128)(2,1)S(1)} reshape(bf16[3,4,16384]{2,1,0:T(4,128)(2,1)} %param.6) | data formatting | bytes 786432 | tf_op jit(solution)/shard_map/reshape | solution.py:327
  1.4 0.0 copy-done.2
  1.4 0.0 copy-start
  1.4 1.2 %copy-done = bf16[128,4096]{1,0:T(8,128)(2,1)S(1)} copy-done((bf16[128,4096]{1,0:T(8,128)(2,1)S(1)}, bf16[128,4096]{1,0:T(8,128)(2,1)}, u32[]{:S(2)}) %copy-start) | copy-done | bytes 1048600
  2.7 0.0 copy-start.1
  2.7 1.2 %copy-done.1 = bf16[128,4096]{1,0:T(8,128)(2,1)S(1)} copy-done((bf16[128,4096]{1,0:T(8,128)(2,1)S(1)}, bf16[128,4096]{1,0:T(8,128)(2,1)}, u32[]{:S(2)}) %copy-start.1) | copy-done | bytes 1048600
  3.9 87.4 %shard_map.46 = f32[3,4,128,128]{3,2,1,0:T(8,128)S(1)} custom-call(s32[2,4,16]{2,1,0:T(4,128)S(1)} %copy-done.2, bf16[128,4096]{1,0:T(8,128)(2,1)S(1)} %copy-done, bf16[128,4096]{1,0:T(8,128)(2,1)S(1)} %copy-done.1, bf16[3,4,128,128]{3,2,1,0:T(8,128)(2,1)S(1)} %reshape.6.w_ref), custom_call_target="tpu_custom_call" | custom-call | tf_op jit(solution)/shard_map/pallas_call | solution.py:329
  91.2 1.2 %reshape.7 = f32[3,4,16384]{2,1,0:T(4,128)} reshape(f32[3,4,128,128]{3,2,1,0:T(8,128)S(1)} %shard_map.46) | data formatting | bytes 1572864 | tf_op jit(solution)/shard_map/reshape | solution.py:369
Async XLA Ops:
  0.0 1.4 %copy-start.2 = (s32[2,4,16]{2,1,0:T(4,128)S(1)}, s32[2,4,16]{2,1,0:T(4,128)}, u32[]{:S(2)}) copy-start(s32[2,4,16]{2,1,0:T(4,128)} %kept_ref.1) | copy-start | bytes 1540
  1.4 1.2 %copy-start = (bf16[128,4096]{1,0:T(8,128)(2,1)S(1)}, bf16[128,4096]{1,0:T(8,128)(2,1)}, u32[]{:S(2)}) copy-start(bf16[128,4096]{1,0:T(8,128)(2,1)} %tok_ref.1) | copy-start | bytes 3145732
  2.7 1.2 %copy-start.1 = (bf16[128,4096]{1,0:T(8,128)(2,1)S(1)}, bf16[128,4096]{1,0:T(8,128)(2,1)}, u32[]{:S(2)}) copy-start(bf16[128,4096]{1,0:T(8,128)(2,1)} %cot_ref.1) | copy-start | bytes 3145732

commit v4 on v3

--- a/solution.py
+++ b/solution.py
@@ -248,15 +248,16 @@
         relay(0, step)
 
     pack(1)
+
+    @pl.loop(0, peers - cores)
+    def _(step):
+        relay(1, step)
+
     crossed(0)
     forward(0)
 
     @pl.loop(0, peers)
     def _(step):
-        @pl.when(step < peers - cores)
-        def _():
-            relay(1, step)
-
         to_pair(0, step)
 
     crossed(1)

time: 92.7 us -> 87.4 us (0.943)
  Pallas kernels: 87.4 us -> 82.1 us
    pallas_call x1, Pallas kernels: 87.4 us -> 82.1 us  [fused(): pl.pallas_call(functools.partial(fused_kernel, n_dp, n_tensor), out_shape...]
where the time goes in v4:
time: 87.4 us; the launch traced here: 87.2 us
  Pallas kernels  82.1 us (94%)
  local copies, waits for them, and re-layouts  5.09 us (6%)
    pallas_call x1, Pallas kernels, fused(): pl.pallas_call(functools.partial(fused_kernel, n_dp, n_tensor), out_shape...  82.1 us
    unnamed x6, local copies, waits for them, and re-layouts  2.45 us

profile of v4, /device:TPU:0, one launch (start us, length us, event | category | flops | bytes accessed | tf_op | source)
XLA Modules:
  0.0 87.2 jit_solution(8991360502917907331)
XLA Ops:
  0.0 0.0 copy-start.2
  0.0 1.4 %reshape.6.w_ref = bf16[3,4,128,128]{3,2,1,0:T(8,128)(2,1)S(1)} reshape(bf16[3,4,16384]{2,1,0:T(4,128)(2,1)} %param.6) | data formatting | bytes 786432 | tf_op jit(solution)/shard_map/reshape | solution.py:328
  1.4 0.0 copy-done.2
  1.4 0.0 copy-start
  1.4 1.2 %copy-done = bf16[128,4096]{1,0:T(8,128)(2,1)S(1)} copy-done((bf16[128,4096]{1,0:T(8,128)(2,1)S(1)}, bf16[128,4096]{1,0:T(8,128)(2,1)}, u32[]{:S(2)}) %copy-start) | copy-done | bytes 1048600
  2.7 0.0 copy-start.1
  2.7 1.2 %copy-done.1 = bf16[128,4096]{1,0:T(8,128)(2,1)S(1)} copy-done((bf16[128,4096]{1,0:T(8,128)(2,1)S(1)}, bf16[128,4096]{1,0:T(8,128)(2,1)}, u32[]{:S(2)}) %copy-start.1) | copy-done | bytes 1048600
  3.9 82.1 %shard_map.46 = f32[3,4,128,128]{3,2,1,0:T(8,128)S(1)} custom-call(s32[2,4,16]{2,1,0:T(4,128)S(1)} %copy-done.2, bf16[128,4096]{1,0:T(8,128)(2,1)S(1)} %copy-done, bf16[128,4096]{1,0:T(8,128)(2,1)S(1)} %copy-done.1, bf16[3,4,128,128]{3,2,1,0:T(8,128)(2,1)S(1)} %reshape.6.w_ref), custom_call_target="tpu_custom_call" | custom-call | tf_op jit(solution)/shard_map/pallas_call | solution.py:330
  86.0 1.2 %reshape.7 = f32[3,4,16384]{2,1,0:T(4,128)} reshape(f32[3,4,128,128]{3,2,1,0:T(8,128)S(1)} %shard_map.46) | data formatting | bytes 1572864 | tf_op jit(solution)/shard_map/reshape | solution.py:370
Async XLA Ops:
  0.0 1.4 %copy-start.2 = (s32[2,4,16]{2,1,0:T(4,128)S(1)}, s32[2,4,16]{2,1,0:T(4,128)}, u32[]{:S(2)}) copy-start(s32[2,4,16]{2,1,0:T(4,128)} %kept_ref.1) | copy-start | bytes 1540
  1.4 1.2 %copy-start = (bf16[128,4096]{1,0:T(8,128)(2,1)S(1)}, bf16[128,4096]{1,0:T(8,128)(2,1)}, u32[]{:S(2)}) copy-start(bf16[128,4096]{1,0:T(8,128)(2,1)} %tok_ref.1) | copy-start | bytes 3145732
  2.7 1.2 %copy-start.1 = (bf16[128,4096]{1,0:T(8,128)(2,1)S(1)}, bf16[128,4096]{1,0:T(8,128)(2,1)}, u32[]{:S(2)}) copy-start(bf16[128,4096]{1,0:T(8,128)(2,1)} %cot_ref.1) | copy-start | bytes 3145732

commit v5 on v4

--- a/solution.py
+++ b/solution.py
@@ -116,6 +116,11 @@
         both_ways(a, mine)
         cross_copy(a, chip, mine).start()
 
+    for a in range(cols):
+        cross_copy(a, chip, mate).wait_recv()
+        both_ways(a, mate)
+        cross_copy(a, chip, mate).start()
+
     def mate_copy(table):
         return pltpu.make_async_remote_copy(
             src_ref=(x_mine, y_mine)[table],
@@ -131,11 +136,6 @@
         for block in range(tiles.shape[0]):
             tiles[block] = src_ref[:, block * BLK : (block + 1) * BLK]
         mate_copy(table).start()
-
-    for a in range(cols):
-        cross_copy(a, chip, mate).wait_recv()
-        both_ways(a, mate)
-        cross_copy(a, chip, mate).start()
 
     def relay(a, step):
         hop = 1 + step // cores
@@ -247,8 +247,6 @@
     def _(step):
         relay(0, step)
 
-    pack(1)
-
     @pl.loop(0, peers - cores)
     def _(step):
         relay(1, step)
@@ -260,6 +258,7 @@
     def _(step):
         to_pair(0, step)
 
+    pack(1)
     crossed(1)
     forward(1)
 

time: 87.4 us -> 87.4 us (level)
  no operation moved by 1% of the time
where the time goes in v5:
time: 87.4 us; the launch traced here: 87.2 us
  Pallas kernels  82.1 us (94%)
  local copies, waits for them, and re-layouts  5.09 us (6%)
    pallas_call x1, Pallas kernels, fused(): pl.pallas_call(functools.partial(fused_kernel, n_dp, n_tensor), out_shape...  82.1 us
    unnamed x6, local copies, waits for them, and re-layouts  2.45 us

profile of v5, /device:TPU:0, one launch (start us, length us, event | category | flops | bytes accessed | tf_op | source)
XLA Modules:
  0.0 87.2 jit_solution(3611250318835887532)
XLA Ops:
  0.0 0.0 copy-start.2
  0.0 1.4 %reshape.6.w_ref = bf16[3,4,128,128]{3,2,1,0:T(8,128)(2,1)S(1)} reshape(bf16[3,4,16384]{2,1,0:T(4,128)(2,1)} %param.6) | data formatting | bytes 786432 | tf_op jit(solution)/shard_map/reshape | solution.py:327
  1.4 0.0 copy-done.2
  1.4 0.0 copy-start
  1.4 1.2 %copy-done = bf16[128,4096]{1,0:T(8,128)(2,1)S(1)} copy-done((bf16[128,4096]{1,0:T(8,128)(2,1)S(1)}, bf16[128,4096]{1,0:T(8,128)(2,1)}, u32[]{:S(2)}) %copy-start) | copy-done | bytes 1048600
  2.7 0.0 copy-start.1
  2.7 1.2 %copy-done.1 = bf16[128,4096]{1,0:T(8,128)(2,1)S(1)} copy-done((bf16[128,4096]{1,0:T(8,128)(2,1)S(1)}, bf16[128,4096]{1,0:T(8,128)(2,1)}, u32[]{:S(2)}) %copy-start.1) | copy-done | bytes 1048600
  3.9 82.1 %shard_map.46 = f32[3,4,128,128]{3,2,1,0:T(8,128)S(1)} custom-call(s32[2,4,16]{2,1,0:T(4,128)S(1)} %copy-done.2, bf16[128,4096]{1,0:T(8,128)(2,1)S(1)} %copy-done, bf16[128,4096]{1,0:T(8,128)(2,1)S(1)} %copy-done.1, bf16[3,4,128,128]{3,2,1,0:T(8,128)(2,1)S(1)} %reshape.6.w_ref), custom_call_target="tpu_custom_call" | custom-call | tf_op jit(solution)/shard_map/pallas_call | solution.py:329
  86.0 1.2 %reshape.7 = f32[3,4,16384]{2,1,0:T(4,128)} reshape(f32[3,4,128,128]{3,2,1,0:T(8,128)S(1)} %shard_map.46) | data formatting | bytes 1572864 | tf_op jit(solution)/shard_map/reshape | solution.py:369
Async XLA Ops:
  0.0 1.4 %copy-start.2 = (s32[2,4,16]{2,1,0:T(4,128)S(1)}, s32[2,4,16]{2,1,0:T(4,128)}, u32[]{:S(2)}) copy-start(s32[2,4,16]{2,1,0:T(4,128)} %kept_ref.1) | copy-start | bytes 1540
  1.4 1.2 %copy-start = (bf16[128,4096]{1,0:T(8,128)(2,1)S(1)}, bf16[128,4096]{1,0:T(8,128)(2,1)}, u32[]{:S(2)}) copy-start(bf16[128,4096]{1,0:T(8,128)(2,1)} %tok_ref.1) | copy-start | bytes 3145732
  2.7 1.2 %copy-start.1 = (bf16[128,4096]{1,0:T(8,128)(2,1)S(1)}, bf16[128,4096]{1,0:T(8,128)(2,1)}, u32[]{:S(2)}) copy-start(bf16[128,4096]{1,0:T(8,128)(2,1)} %cot_ref.1) | copy-start | bytes 3145732
